TPU v7x, 32 devices: a whole 2x2x4 slice. The times are simulated.
32 devices in a mesh: pole: 2 (over y), row: 4 (over z), col: 4 (over x, core).
Axes of the slice: x: 2, y: 2, z: 4, core: 2. Of those that a mesh axis runs over, the one named last changes fastest.
Arguments:
- root_inverse: float32 [8192, 4096], P(('pole', 'row'), 'col'), parts along dimension 0, as said below
- root_factor_one: float32 [8192, 1024], P(('pole', 'row'), 'col'), parts along dimension 0, may hold values from -0.09375 to 0.09375
- diag_inverse_one: float32 [8, 256, 256], P(('pole', 'col')), parts along dimension 0
- root_factor_two: float32 [8192, 2048], P(('pole', 'row'), 'col'), parts along dimension 0, may hold values from -0.09375 to 0.09375
- parent_factor: float32 [16, 256, 256], P(('pole', 'col')), parts along dimension 0, may hold values from -0.109375 to 0.109375
- diag_inverse_two: float32 [16, 256, 256], P(('pole', 'col')), parts along dimension 0
- root_mask_one: int32 [4, 16], replicated, may hold values from 0 to 1, as said below
- root_mask_two: int32 [8, 16], replicated, may hold values from 0 to 1, as said below
- parents: int32 [8], replicated, may hold values from 0 to 3, as said below
Outputs:
- inverse_one: float32 [8192, 1024], P(('pole', 'row'), 'col'), parts along dimension 0
- diag_one: float32 [8, 256, 256], P(('pole', 'col')), parts along dimension 0
- inverse_two: float32 [8192, 2048], P(('pole', 'row'), 'col'), parts along dimension 0
- parent_block: float32 [16, 256, 256], P(('pole', 'col')), parts along dimension 0
- diag_two: float32 [16, 256, 256], P(('pole', 'col')), parts along dimension 0
There are 2 independent parts, one for each index of `pole`. A program takes and returns all parts, laid end to end along the dimension named above; an argument that names none is the same for every part. Nothing has to cross between parts.
Inputs may be any that keep to these rules, and one draw needn't show every extreme that they name: `root_inverse`: symmetric. `root_mask_one`: 1 where root supernode b belongs to the structure of level-one supernode k. `root_mask_two`: 1 only where the same root supernode is 1 for the parent parents[k] in root_mask_one. `parents`: every level-one supernode is the parent of at least one level-two supernode.
All inputs are finite; a program needn't handle non-finite values.
Results may differ from a plain program's by a relative error of at most 0.000073.
Values sent between devices are 32-bit elements; how exact they have to be, the bound alone decides.
A program may use at most 128 MiB of HBM per device.

v0:
```python
import jax
import jax.numpy as jnp
from jax import lax
from jax.sharding import PartitionSpec as P


def on_device(
    root_inverse,
    root_factor_one,
    diag_inverse_one,
    root_factor_two,
    parent_factor,
    diag_inverse_two,
    root_mask_one,
    root_mask_two,
    parents,
):
    highest = lax.Precision.HIGHEST
    block_width = parent_factor.shape[1]
    local_rows = root_inverse.shape[0]
    per_one = diag_inverse_one.shape[0]
    per_two = diag_inverse_two.shape[0]
    root_blocks = root_mask_one.shape[1]
    row_start = lax.axis_index("row") * local_rows
    col_index = lax.axis_index("col")
    block_of = (row_start + jnp.arange(local_rows, dtype=jnp.int32)) // block_width
    onehot = (block_of[:, None] == jnp.arange(root_blocks, dtype=jnp.int32)[None, :]).astype(
        jnp.float32
    )

    def row_masks(mask, number):
        own_mask = lax.dynamic_slice_in_dim(mask, col_index * number, number, 0).astype(jnp.float32)
        return jnp.dot(onehot, own_mask.T, precision=highest)[:, :, None]

    mask_one = row_masks(root_mask_one, per_one)
    mask_two = row_masks(root_mask_two, per_two)
    factor_one = root_factor_one.reshape(local_rows, per_one, block_width) * mask_one
    factor_two = root_factor_two.reshape(local_rows, per_two, block_width) * mask_two
    flat_one = factor_one.reshape(local_rows, per_one * block_width)
    flat_two = factor_two.reshape(local_rows, per_two * block_width)
    panel = lax.all_gather(root_inverse, "col", axis=1, tiled=True)

    def partial_terms(flat):
        return lax.dot_general(
            panel,
            flat,
            (((0,), (0,)), ((), ())),
            precision=highest,
            preferred_element_type=jnp.float32,
        )

    sum_one = lax.psum_scatter(partial_terms(flat_one), "row", scatter_dimension=0, tiled=True)
    sum_two = lax.psum_scatter(partial_terms(flat_two), "row", scatter_dimension=0, tiled=True)
    inverse_one = -sum_one.reshape(local_rows, per_one, block_width) * mask_one
    diag_part = jnp.einsum("ikw,ikv->kwv", factor_one, inverse_one, precision=highest)
    diag_one = diag_inverse_one - lax.psum(diag_part, "row")
    own_parents = lax.dynamic_slice_in_dim(parents, col_index * per_two, per_two, 0)
    all_inverse, all_diag = (
        lax.all_gather(inverse_one, "col", axis=1, tiled=True),
        lax.all_gather(diag_one, "col", axis=0, tiled=True),
    )
    parent_cols = jnp.take(all_inverse, own_parents, axis=1)
    parent_diag = jnp.take(all_diag, own_parents, axis=0)
    cross_term = jnp.einsum("ikw,kwv->ikv", parent_cols, parent_factor, precision=highest)
    parent_part = jnp.einsum("ikw,ikv->kwv", parent_cols, factor_two, precision=highest)
    inverse_two = -(sum_two.reshape(local_rows, per_two, block_width) + cross_term) * mask_two
    diag_part_two = jnp.einsum("ikw,ikv->kwv", factor_two, inverse_two, precision=highest)
    summed_parent, summed_diag = lax.psum((parent_part, diag_part_two), "row")
    parent_block = -(
        summed_parent + jnp.einsum("kwv,kvx->kwx", parent_diag, parent_factor, precision=highest)
    )
    diag_two = (
        diag_inverse_two
        - summed_diag
        - jnp.einsum("kwv,kwx->kvx", parent_factor, parent_block, precision=highest)
    )
    return (
        inverse_one.reshape(local_rows, per_one * block_width),
        diag_one,
        inverse_two.reshape(local_rows, per_two * block_width),
        parent_block,
        diag_two,
    )


def solution(mesh):
    in_specs = (
        P(("pole", "row"), "col"),
        P(("pole", "row"), "col"),
        P(("pole", "col"), None, None),
        P(("pole", "row"), "col"),
        P(("pole", "col"), None, None),
        P(("pole", "col"), None, None),
        P(),
        P(),
        P(),
    )
    out_specs = (
        P(("pole", "row"), "col"),
        P(("pole", "col"), None, None),
        P(("pole", "row"), "col"),
        P(("pole", "col"), None, None),
        P(("pole", "col"), None, None),
    )
    return jax.shard_map(
        on_device, mesh=mesh, in_specs=in_specs, out_specs=out_specs, check_vma=False
    )
```

profile of v0, /device:TPU:0, one launch (start us, length us, event | category | flops | bytes accessed | tf_op | source)
XLA Modules:
  0.0 499.3 jit_solution(6730628027769771489)
XLA Ops:
  7.2 0.7 all-gather.5.cloned.1.call-update
  8.0 0.5 copy-done.6
  8.5 0.3 copy.25
  8.8 1.2 fusion.28
  10.0 108.2 %all-gather.5.cloned.1.call-done = f32[1024,4096]{1,0:T(8,128)} async-done(((f32[1024,1024]{1,0:T(8,128)}), f32[1024,4096]{1,0:T(8,128)}) %all-gather.5.cloned.1.call-update) | async-done | bytes 16777232 | tf_op jit(solution)/shard_map/all_gather | solution.py:41
  118.2 18.0 %convolution_bitcast_fusion.1 = f32[4096,256]{0,1:T(8,128)} fusion(f32[1024,4096]{1,0:T(8,128)} %all-gather.5.cloned.1.call-done, f32[1024,256]{0,1:T(8,128)S(1)} %copy.25, f32[1024]{0:T(1024)S(1)} %bitcast.46), kind=kOutput, calls=%fused_computation.3 | convolution fusion | flops 12885164032 | bytes 22024192 | tf_op jit(solution)/shard_map/dot_general | solution.py:44
  136.3 0.0 all-gather.9.cloned.1.call-start
  136.3 76.9 %reduce-scatter.3.cloned.1.call-done = f32[1024,256]{0,1:T(8,128)} async-done(((f32[4096,256]{0,1:T(8,128)}), f32[1024,256]{0,1:T(8,128)}) %reduce-scatter.3.cloned.1.call-update) | async-done | bytes 1048592 | tf_op jit(solution)/shard_map/reduce_scatter | solution.py:52
  213.2 2.4 negate_multiply_fusion
  215.6 0.2 reduce-scatter.5.cloned.1.call-start
  215.8 1.1 fusion.27
  217.0 1.6 mul.49
  218.6 3.0 copy.26
  221.6 32.3 %convolution_bitcast_fusion = f32[4096,512]{0,1:T(8,128)} fusion(f32[1024,4096]{1,0:T(8,128)} %all-gather.5.cloned.1.call-done, f32[1024,512]{1,0:T(8,128)S(1)} %copy-done.4, f32[1024,512]{1,0:T(8,128)} %copy.26), kind=kOutput, calls=%fused_computation.2 | convolution fusion | flops 25770328064 | bytes 29360128 | tf_op jit(solution)/shard_map/dot_general | solution.py:44
  253.9 0.3 all-reduce.3.cloned.1.call-start
  254.2 1.9 copy.29
  256.1 0.1 compare_and_fusion
  256.2 3.3 convolution_bitcast_fusion.3
  259.6 4.9 gather_fusion
  264.5 4.6 fusion.2
  269.1 129.9 %reduce-scatter.5.cloned.1.call-done = f32[1024,512]{0,1:T(8,128)} async-done(((f32[4096,512]{0,1:T(8,128)}), f32[1024,512]{0,1:T(8,128)}) %reduce-scatter.5.cloned.1.call-update) | async-done | bytes 2097168 | tf_op jit(solution)/shard_map/reduce_scatter | solution.py:53
  399.0 4.6 fusion.1
  403.6 1.3 copy-done.1
  405.0 3.0 fusion.9
  408.0 61.6 %all-reduce.3.cloned.1.call-done = (f32[1,256,256]{2,1,0:T(8,128)}, f32[2,256,256]{2,1,0:T(8,128)}, f32[2,256,256]{2,1,0:T(8,128)}) async-done(((f32[1,256,256]{2,1,0:T(8,128)}, f32[2,256,256]{2,1,0:T(8,128)}, f32[2,256,256]{2,1,0:T(8,128)}), (f32[1,256,256]{2,1,0:T(8,128)}, f32[2,256,256]{2,1,0:T(8,128)}, f32[2,256,256]{2,1,0:T(8,128)})) %all-reduce.3.cloned.1.call-update) | async-done | bytes 1310736 | tf_op jit(solution)/shard_map/psum | solution.py:56
  469.6 1.7 sub.16
  471.3 2.5 copy.34
  473.8 1.8 copy.35
  475.6 12.4 %all-gather.7.cloned.1.call-done = f32[4,256,256]{2,1,0:T(8,128)} async-done(((f32[1,256,256]{2,1,0:T(8,128)}), f32[4,256,256]{2,1,0:T(8,128)}) %all-gather.7.cloned.1.call-update) | async-done | bytes 1048592 | tf_op jit(solution)/shard_map/all_gather | solution.py:60
  488.0 1.8 gather_fusion.1
  489.9 0.7 fusion.14
  490.6 1.9 fusion.15
  (33 shorter events, 0.3 us)
Async XLA Ops:
  7.2 391.8 %copy-start = (f32[2,256,256]{2,1,0:T(8,128)S(1)}, f32[2,256,256]{2,1,0:T(8,128)}, u32[]{:S(2)}) copy-start(f32[2,256,256]{2,1,0:T(8,128)} %param.13) | copy-start | bytes 1572868
  7.2 1.3 copy-start.6
  7.2 111.0 %all-gather.5.cloned.1.call-start = ((), (), s32[]{:S(2)}) async-start(), calls=%async_computation.2 | async-start | bytes 20971520 | tf_op jit(solution)/shard_map/all_gather | solution.py:41
  7.9 205.3 %reduce-scatter.3.cloned.1.call-start = ((), (), s32[]{:S(2)}) async-start(), calls=%async_computation.3 | async-start | bytes 5242880 | tf_op jit(solution)/shard_map/reduce_scatter | solution.py:52
  8.8 127.5 %copy-start.3 = (f32[1024,256]{0,1:T(8,128)}, f32[1024,256]{0,1:T(8,128)S(1)}, u32[]{:S(2)}) copy-start(f32[1024,256]{0,1:T(8,128)S(1)} %copy.25) | copy-start | bytes 3145732
  136.3 123.3 %all-gather.9.cloned.1.call-start = ((), (), s32[]{:S(2)}) async-start(), calls=%async_computation.6 | async-start | bytes 5242880 | tf_op jit(solution)/shard_map/all_gather | solution.py:59
  215.6 183.4 %reduce-scatter.5.cloned.1.call-start = ((), (), s32[]{:S(2)}) async-start(), calls=%async_computation.4 | async-start | bytes 10485760 | tf_op jit(solution)/shard_map/reduce_scatter | solution.py:53
  218.6 3.1 copy-start.4
  253.9 2.2 copy-start.11
  253.9 215.7 %all-reduce.3.cloned.1.call-start = ((), (), s32[]{:S(2)}) async-start(), calls=%async_computation.7 | async-start | bytes 2621440 | tf_op jit(solution)/shard_map/psum | solution.py:56
  403.6 1.3 copy-start.1
  405.0 64.6 %copy-start.10 = (f32[1,256,256]{2,1,0:T(8,128)S(1)}, f32[1,256,256]{2,1,0:T(8,128)}, u32[]{:S(2)}) copy-start(f32[1,256,256]{2,1,0:T(8,128)} %param.11) | copy-start | bytes 786436
  407.9 65.9 %copy-start.2 = (f32[1024,2,256]{0,2,1:T(8,128)S(1)}, f32[1024,2,256]{0,2,1:T(8,128)}, u32[]{:S(2)}) copy-start(f32[1024,2,256]{0,2,1:T(8,128)} %copy-done.1) | copy-start | bytes 6291460
  408.0 80.1 %all-gather.7.cloned.1.call-start = ((), (), s32[]{:S(2)}) async-start(), calls=%async_computation.5 | async-start | bytes 1310720 | tf_op jit(solution)/shard_map/all_gather | solution.py:60
  473.8 16.0 %copy-start.9 = (f32[2,256,256]{2,1,0:T(8,128)S(1)}, f32[2,256,256]{2,1,0:T(8,128)}, u32[]{:S(2)}) copy-start(f32[2,256,256]{2,1,0:T(8,128)} %get-tuple-element.16) | copy-start | bytes 1572868
  475.6 14.9 %copy-start.7 = (f32[2,256,256]{2,1,0:T(8,128)S(1)}, f32[2,256,256]{2,1,0:T(8,128)}, u32[]{:S(2)}) copy-start(f32[2,256,256]{2,1,0:T(8,128)} %param.14) | copy-start | bytes 1572868
  475.6 14.9 %copy-start.8 = (f32[2,256,256]{2,1,0:T(8,128)S(1)}, f32[2,256,256]{2,1,0:T(8,128)}, u32[]{:S(2)}) copy-start(f32[2,256,256]{2,1,0:T(8,128)} %get-tuple-element.17) | copy-start | bytes 1572868
  490.5 1.9 copy-start.5
Sparse Core Ops, SparseCore 0:
  9.6 108.6 all-gather.4
  136.4 76.7 reduce-scatter.2
  215.7 34.9 all-gather.8
  254.0 144.9 reduce-scatter.4
  408.1 61.4 all-reduce.2
  471.6 16.3 all-gather.6
where the time goes:
time: 500 us; the launch traced here: 499 us
  waiting for transfers between devices  390 us (78%)
  matrix products  70.6 us (14%)
  local copies, waits for them, and re-layouts  19.8 us (4%)
  between operations  14.3 us (3%)
    reduce_scatter x1, waiting for transfers between devices, on_device(): lax.psum_scatter(partial_terms(flat_two), 'row', scatter_dimension=0, til...  130 us
    all_gather x1, waiting for transfers between devices, on_device(): panel = lax.all_gather(root_inverse, 'col', axis=1, tiled=True)  108 us
    reduce_scatter x1, waiting for transfers between devices, on_device(): lax.psum_scatter(partial_terms(flat_one), 'row', scatter_dimension=0, til...  76.9 us
    psum x1, waiting for transfers between devices, on_device(): diag_one = diag_inverse_one - lax.psum(diag_part, 'row')  61.6 us
    dot_general x2, matrix products, partial_terms(): lax.dot_general(panel, flat, (((0,), (0,)), ((), ())), precision=highest,...  50.3 us
    all_gather x1, waiting for transfers between devices, on_device(): lax.all_gather(diag_one, 'col', axis=0, tiled=True)  12.4 us
  transfers between devices with their start and end apart: 6, of which 5 were waited for; matrix products, arithmetic and copies ran while one was open for 12% of the time, Pallas kernels for 0%

commit v1 on v0

v1 whole, which is shorter than its diff:
```python
import functools

import jax
import jax.numpy as jnp
from jax import lax
from jax.experimental import pallas as pl
from jax.experimental.pallas import tpu as pltpu
from jax.sharding import PartitionSpec as P

HIGH = lax.Precision.HIGH


MESH = pl.DeviceIdType.MESH
CHUNKS = 4


def gather_kernel(
    rows_n, chips, a_ref, f_ref, panel, whole, f_send, f_recv, x_send, x_recv, s_send, s_recv, own
):
    row, col = lax.axis_index("row"), lax.axis_index("col")
    core, chip = lax.rem(col, 2), col // 2
    sibling = chip * 2 + 1 - core
    height, wide = a_ref.shape
    step = height // CHUNKS
    tall = f_ref.shape[0]

    barrier = pltpu.get_barrier_semaphore()
    for s in range(1, rows_n):
        pl.semaphore_signal(
            barrier, inc=1, device_id={"row": lax.rem(row + s, rows_n)}, device_id_type=MESH
        )
    for d in range(1, chips):
        other = lax.rem(chip + d, chips) * 2 + core
        pl.semaphore_signal(barrier, inc=1, device_id={"col": other}, device_id_type=MESH)
    pl.semaphore_signal(barrier, inc=1, device_id={"col": sibling}, device_id_type=MESH)
    pl.semaphore_wait(barrier, rows_n + chips - 1)

    def slot(c, ch):
        return panel.at[pl.ds(ch * step, step), pl.ds(pl.multiple_of(c * wide, wide), wide)]

    def across(d, ch):
        return pltpu.make_async_remote_copy(
            src_ref=a_ref.at[pl.ds(ch * step, step)],
            dst_ref=slot(col, ch),
            send_sem=x_send.at[d - 1, ch],
            recv_sem=x_recv.at[d - 1, ch],
            device_id={"col": lax.rem(chip + d, chips) * 2 + core},
            device_id_type=MESH,
        )

    def beside(d, ch):
        source = lax.rem(chip + chips - d, chips) * 2 + core
        src = a_ref.at[pl.ds(ch * step, step)] if d == 0 else slot(source, ch)
        return pltpu.make_async_remote_copy(
            src_ref=src,
            dst_ref=slot(source, ch),
            send_sem=s_send.at[d, ch],
            recv_sem=s_recv.at[d, ch],
            device_id={"col": sibling},
            device_id_type=MESH,
        )

    def place(r):
        return whole.at[pl.ds(pl.multiple_of(r * tall, tall), tall)]

    copies = []
    for ch in range(CHUNKS):
        for d in range(1, chips):
            c = across(d, ch)
            c.start()
            copies.append(c)
    sends = []
    for s in range(1, rows_n):
        c = pltpu.make_async_remote_copy(
            src_ref=f_ref,
            dst_ref=place(row),
            send_sem=f_send.at[s - 1],
            recv_sem=f_recv.at[s - 1],
            device_id={"row": lax.rem(row + s, rows_n)},
            device_id_type=MESH,
        )
        c.start()
        sends.append(c)
    local_f = pltpu.make_async_copy(f_ref, place(row), own.at[0])
    local_f.start()
    local_a = pltpu.make_async_copy(
        a_ref, panel.at[:, pl.ds(pl.multiple_of(col * wide, wide), wide)], own.at[1]
    )
    local_a.start()
    forwards = []
    for ch in range(CHUNKS):
        c = beside(0, ch)
        c.start()
        forwards.append(c)
    at = 0
    for ch in range(CHUNKS):
        for d in range(1, chips):
            copies[at].wait_recv()
            at += 1
            c = beside(d, ch)
            c.start()
            forwards.append(c)
    for c in copies:
        c.wait_send()
    for c in forwards:
        c.wait()
    for c in sends:
        c.wait()
    local_f.wait()
    local_a.wait()


def gather_first(a, f, rows_n, cols_n):
    chips = cols_n // 2
    dma = pltpu.SemaphoreType.DMA
    return pl.pallas_call(
        functools.partial(gather_kernel, rows_n, chips),
        out_shape=(
            jax.ShapeDtypeStruct((a.shape[0], cols_n * a.shape[1]), a.dtype),
            jax.ShapeDtypeStruct((rows_n * f.shape[0], f.shape[1]), f.dtype),
        ),
        in_specs=[pl.BlockSpec(memory_space=pl.ANY)] * 2,
        out_specs=(pl.BlockSpec(memory_space=pl.ANY),) * 2,
        scratch_shapes=[
            dma((rows_n - 1,)),
            dma((rows_n - 1,)),
            dma((chips - 1, CHUNKS)),
            dma((chips - 1, CHUNKS)),
            dma((chips, CHUNKS)),
            dma((chips, CHUNKS)),
            dma((2,)),
        ],
        compiler_params=pltpu.CompilerParams(collective_id=0, has_side_effects=True),
    )(a, f)


def permuted(block, count):
    return [
        lax.ppermute(block, "row", [(i, (i + shift) % count) for i in range(count)])
        for shift in range(1, count)
    ]


def assemble(whole, block, pieces, count, index, column):
    rows = block.shape[0]
    for shift, piece in enumerate([block] + pieces):
        owner = lax.rem(index + count - shift, count)
        whole = lax.dynamic_update_slice(whole, piece, (owner * rows, jnp.int32(column)))
    return whole


def on_device(
    root_inverse,
    root_factor_one,
    diag_inverse_one,
    root_factor_two,
    parent_factor,
    diag_inverse_two,
    root_mask_one,
    root_mask_two,
    parents,
    row_count,
    col_count,
):
    width = parent_factor.shape[1]
    local_rows = root_inverse.shape[0]
    per_one = diag_inverse_one.shape[0]
    per_two = diag_inverse_two.shape[0]
    row_index = lax.axis_index("row")
    col_index = lax.axis_index("col")
    blocks = local_rows // width

    def row_masks(mask, number):
        own = lax.dynamic_slice(mask, (col_index * number, row_index * blocks), (number, blocks))
        return jnp.repeat(own.T.astype(jnp.float32), width, axis=0)

    mask_one = row_masks(root_mask_one, per_one)
    mask_two = row_masks(root_mask_two, per_two)
    one = [
        root_factor_one[:, k * width : (k + 1) * width] * mask_one[:, k : k + 1]
        for k in range(per_one)
    ]
    two = [
        root_factor_two[:, k * width : (k + 1) * width] * mask_two[:, k : k + 1]
        for k in range(per_two)
    ]
    half = width // 2
    early = jnp.concatenate(one + [two[0][:, :half]], axis=1)
    panel, whole_early = gather_first(root_inverse, early, row_count, col_count)
    late = [two[0][:, half:]] + two[1:]
    panel, late = lax.optimization_barrier((panel, late))
    pieces = [permuted(f, row_count) for f in late]
    whole_one = [whole_early[:, k * width : (k + 1) * width] for k in range(per_one)]
    start = jnp.pad(whole_early[:, per_one * width :], ((0, 0), (0, half)))
    whole_two = [assemble(start, late[0], pieces[0], row_count, row_index, half)]

    def dot(a, b):
        return jnp.dot(a, b, precision=HIGH, preferred_element_type=jnp.float32)

    def dot_t(a, b):
        return lax.dot_general(
            a, b, (((0,), (0,)), ((), ())), precision=HIGH, preferred_element_type=jnp.float32
        )

    inv_one = [-dot(panel, whole_one[k]) * mask_one[:, k : k + 1] for k in range(per_one)]
    inverse_one = jnp.concatenate(inv_one, axis=1) if per_one > 1 else inv_one[0]
    diag_part = jnp.stack([dot_t(one[k], inv_one[k]) for k in range(per_one)])
    own_parents = lax.dynamic_slice_in_dim(parents, col_index * per_two, per_two, 0)
    all_inverse = lax.all_gather(inverse_one, "col", axis=0, tiled=False)

    parent_cols = []
    for k in range(per_two):
        p = own_parents[k]
        wide = lax.dynamic_index_in_dim(all_inverse, p // per_one, 0, keepdims=False)
        parent_cols.append(lax.dynamic_slice_in_dim(wide, (p % per_one) * width, width, 1))
    parent_part = jnp.stack([dot_t(parent_cols[k], two[k]) for k in range(per_two)])
    summed_one, summed_parent = lax.psum((diag_part, parent_part), "row")
    diag_one = diag_inverse_one - summed_one
    all_diag = lax.all_gather(diag_one, "col", axis=0, tiled=True)
    parent_block, inv_two, diag_two = [], [], []
    for k in range(per_two):
        parent_diag = lax.dynamic_index_in_dim(all_diag, own_parents[k], 0, keepdims=False)
        parent_block.append(-(summed_parent[k] + dot(parent_diag, parent_factor[k])))
        cross = dot(parent_cols[k], parent_factor[k])
        if k == 0:
            total = dot(panel, whole_two[0]) + cross
        else:
            total = cross
            for shift, piece in enumerate([late[k]] + pieces[k]):
                owner = lax.rem(row_index + row_count - shift, row_count)
                columns = lax.dynamic_slice_in_dim(panel, owner * local_rows, local_rows, 1)
                total = total + dot(columns, piece)
        inv_two.append(-total * mask_two[:, k : k + 1])
    diag_part_two = jnp.stack([dot_t(two[k], inv_two[k]) for k in range(per_two)])
    diag_part_two, parent_block = lax.optimization_barrier((diag_part_two, parent_block))
    summed_diag = lax.psum(diag_part_two, "row")
    diag_two = [
        diag_inverse_two[k] - summed_diag[k] - dot_t(parent_factor[k], parent_block[k])
        for k in range(per_two)
    ]
    return (
        inverse_one,
        diag_one,
        jnp.concatenate(inv_two, axis=1),
        jnp.stack(parent_block),
        jnp.stack(diag_two),
    )


def solution(mesh):
    row_count, col_count = mesh.shape["row"], mesh.shape["col"]
    tall = P(("pole", "row"), "col")
    deep = P(("pole", "col"), None, None)

    def step(*args):
        return on_device(*args, row_count, col_count)

    return jax.shard_map(
        step,
        mesh=mesh,
        in_specs=(tall, tall, deep, tall, deep, deep, P(), P(), P()),
        out_specs=(tall, deep, tall, deep, deep),
        check_vma=False,
    )
```

time: 500 us -> 468 us (0.936)
  waiting for transfers between devices: 390 us -> 168 us
  Pallas kernels: 0 us -> 181 us
  starting transfers between devices: 0.64 us -> 10.1 us
  matrix products: 70.6 us -> 62 us
  other arithmetic: 4.16 us -> 11.6 us
    reduce_scatter x2 -> x0, waiting for transfers between devices: 207 us -> none  [the longest x1 130 us: on_device(): lax.psum_scatter(partial_terms(flat_two), 'row', scatter_dimension=0, til...]
    pallas_call x0 -> x1, Pallas kernels: none -> 181 us  [gather_first(): pl.pallas_call(functools.partial(gather_kernel, rows_n, chips), out_shape...]
    all_gather x3 -> x2, waiting for transfers between devices: 121 us -> 1.47 us  [the longest x1 1.47 us: on_device(): all_diag = lax.all_gather(diag_one, 'col', axis=0, tiled=True)]
    ppermute x0 -> x6, waiting for transfers between devices: none -> 101 us  [permuted(): lax.ppermute(block, 'row', [(i, (i + shift) % count) for i in range(count)])]
    ppermute x0 -> x6, starting transfers between devices: none -> 9.74 us  [permuted(): lax.ppermute(block, 'row', [(i, (i + shift) % count) for i in range(count)])]
    dot_general x10 -> x17, matrix products: 70.6 us -> 62 us  [the longest x10 50.9 us: dot(): return jnp.dot(a, b, precision=HIGH, preferred_element_type=jnp.float32)]
    dynamic_update_slice x0 -> x4, local copies, waits for them, and re-layouts: none -> 7.56 us  [assemble(): lax.dynamic_update_slice(whole, piece, (owner * rows, jnp.int32(column)))]
    unnamed x28 -> x24, local copies, waits for them, and re-layouts: 8.44 us -> 1.21 us
  transfers between devices with their start and end apart: 6 -> 10, of which waited for: 5 -> 6; matrix products, arithmetic and copies ran while one was open for 12% -> 14% of each run, Pallas kernels for 0% -> 0%
where the time goes in v1:
time: 468 us
  Pallas kernels  181 us (39%)
  waiting for transfers between devices  168 us (36%)
  matrix products  62 us (13%)
  between operations  18 us (4%)
  local copies, waits for them, and re-layouts  17.3 us (4%)
  other arithmetic  11.6 us (2%)
  starting transfers between devices  10.1 us (2%)
    pallas_call x1, Pallas kernels, gather_first(): pl.pallas_call(functools.partial(gather_kernel, rows_n, chips), out_shape...  181 us
    ppermute x6, waiting for transfers between devices, permuted(): lax.ppermute(block, 'row', [(i, (i + shift) % count) for i in range(count)])  101 us
    dot_general x10, matrix products, dot(): return jnp.dot(a, b, precision=HIGH, preferred_element_type=jnp.float32)  50.9 us
    psum x1, waiting for transfers between devices, on_device(): summed_diag = lax.psum(diag_part_two, 'row')  36 us
    psum x1, waiting for transfers between devices, on_device(): summed_one, summed_parent = lax.psum((diag_part, parent_part), 'row')  28.8 us
    dot_general x7, matrix products, dot_t(): lax.dot_general(a, b, (((0,), (0,)), ((), ())), precision=HIGH, preferred...  11 us
    ppermute x6, starting transfers between devices, permuted(): lax.ppermute(block, 'row', [(i, (i + shift) % count) for i in range(count)])  9.74 us
  transfers between devices with their start and end apart: 10, of which 6 were waited for; matrix products, arithmetic and copies ran while one was open for 14% of the time, Pallas kernels for 0%

profile of v1, /device:TPU:0, one launch (start us, length us, event | category | flops | bytes accessed | tf_op | source)
XLA Modules:
  0.0 467.6 jit_solution(3718324378717237724)
XLA Ops:
  9.0 1.9 slice_multiply_fusion
  14.2 181.1 %shard_map.128 = (f32[1024,4096]{1,0:T(8,128)}, f32[4096,384]{1,0:T(8,128)}) custom-call(f32[1024,1024]{1,0:T(8,128)} %a_ref.1, f32[1024,384]{1,0:T(8,128)} %pad_maximum_fusion.1.f_ref), custom_call_target="tpu_custom_call" | custom-call | tf_op jit(solution)/shard_map/pallas_call | solution.py:116
  195.4 12.4 %fusion.13 = f32[1024,256]{1,0:T(8,128)} fusion(f32[1024,4096]{1,0:T(8,128)} %get-tuple-element.14, f32[4096,384]{1,0:T(8,128)} %get-tuple-element.15, f32[1024]{0:T(1024)S(1)} %bitcast.115), kind=kOutput, calls=%fused_computation.13 | convolution fusion | flops 6442975232 | bytes 22024192 | tf_op jit(solution)/shard_map/dot_general | solution.py:198
  207.9 1.5 collective-permute-start.5
  209.9 3.3 collective-permute-start.2
  213.2 2.9 collective-permute-start.4
  219.4 3.1 slice.69
  223.9 3.9 pad.4
  227.8 1.9 constant_dynamic-update-slice_fusion.3
  229.7 1.7 convolution_bitcast_fusion.6
  231.4 13.9 %collective-permute-done = f32[1024,128]{1,0:T(8,128)} collective-permute-done((f32[1024,128]{1,0:T(8,128)}, f32[1024,128]{1,0:T(8,128)}, u32[]{:S(2)}, u32[]{:S(2)}) %collective-permute-start) | collective-permute-done | bytes 524320 | tf_op jit(solution)/shard_map/ppermute | solution.py:139
  245.4 1.4 collective-permute-start.3
  246.8 1.9 constant_dynamic-update-slice_fusion.2
  248.7 75.3 %collective-permute-done.1 = f32[1024,128]{1,0:T(8,128)} collective-permute-done((f32[1024,128]{1,0:T(8,128)}, f32[1024,128]{1,0:T(8,128)}, u32[]{:S(2)}, u32[]{:S(2)}) %collective-permute-start.1) | collective-permute-done | bytes 524320 | tf_op jit(solution)/shard_map/ppermute | solution.py:139
  324.0 1.9 constant_dynamic-update-slice_fusion.1
  325.9 1.9 constant_dynamic-update-slice_fusion
  327.8 5.3 %fusion = f32[1024,256]{1,0:T(8,128)} fusion(f32[1024,256]{1,0:T(8,128)} %collective-permute-done.5, f32[1024,4096]{1,0:T(8,128)} %get-tuple-element.14, s32[]{:T(128)S(6)} %select_n.55), kind=kOutput, calls=%fused_computation | convolution fusion | flops 1610612736 | bytes 6291460 | tf_op jit(solution)/shard_map/dot_general | solution.py:198
  333.0 12.0 %collective-permute-done.4 = f32[1024,256]{1,0:T(8,128)} collective-permute-done((f32[1024,256]{1,0:T(8,128)S(1)}, f32[1024,256]{1,0:T(8,128)}, u32[]{:S(2)}, u32[]{:S(2)}) %collective-permute-start.4) | collective-permute-done | bytes 1048608 | tf_op jit(solution)/shard_map/ppermute | solution.py:139
  345.0 5.3 %fusion.2 = f32[1024,256]{1,0:T(8,128)} fusion(f32[1024,256]{1,0:T(8,128)} %collective-permute-done.4, f32[1024,4096]{1,0:T(8,128)} %get-tuple-element.14, s32[]{:T(128)S(6)} %select_n.54), kind=kOutput, calls=%fused_computation.2 | convolution fusion | flops 1610612736 | bytes 6291460 | tf_op jit(solution)/shard_map/dot_general | solution.py:198
  350.3 2.3 convolution_bitcast_fusion.3
  352.5 2.2 convolution_bitcast_fusion.2
  355.7 2.8 fusion.46
  358.5 1.9 fusion.43
  360.4 4.2 fusion.16
  364.7 4.5 fusion.31
  369.2 28.8 %all-reduce.7.cloned.1.call-done = (f32[1,256,256]{2,1,0:T(8,128)}, f32[2,256,256]{2,1,0:T(8,128)}) async-done(((f32[1,256,256]{2,1,0:T(8,128)}, f32[2,256,256]{2,1,0:T(8,128)}), (f32[1,256,256]{2,1,0:T(8,128)}, f32[2,256,256]{2,1,0:T(8,128)})) %all-reduce.7.cloned.1.call-update) | async-done | bytes 786448 | tf_op jit(solution)/shard_map/psum | solution.py:217
  398.0 1.7 sub.36
  401.0 11.8 %fusion.35 = f32[1024,256]{1,0:T(8,128)S(1)} fusion(f32[1024,256]{1,0:T(8,128)} %fusion.46, f32[1024,4096]{1,0:T(8,128)} %get-tuple-element.14, f32[4096,256]{1,0:T(8,128)} %constant_dynamic-update-slice_fusion, f32[1024]{0:T(1024)S(1)} %bitcast.117), kind=kOutput, calls=%fused_computation.22 | convolution fusion | flops 6443237376 | bytes 23072768 | tf_op jit(solution)/shard_map/dot_general | solution.py:198
  414.6 1.5 all-gather.4.cloned.1.call-done
  418.9 1.6 pad_maximum_fusion
  421.4 36.0 %all-reduce.5.cloned.1.call-done = f32[2,256,256]{2,1,0:T(8,128)} async-done(((f32[2,256,256]{2,1,0:T(8,128)}), f32[2,256,256]{2,1,0:T(8,128)}) %all-reduce.5.cloned.1.call-update) | async-done | bytes 524304 | tf_op jit(solution)/shard_map/psum | solution.py:236
  458.8 1.4 fusion.39
  (55 shorter events, 16.3 us)
Async XLA Ops:
  7.2 4.6 copy-start.7
  7.2 343.1 %all-gather.6.cloned.1.call-start = ((), (), s32[]{:S(2)}) async-start(), calls=%async_computation.2 | async-start | bytes 5242880 | tf_op jit(solution)/shard_map/all_gather | solution.py:209
  12.0 1.0 copy-start.1
  195.4 20.8 %copy-start.9 = (s32[8]{0:T(128)S(1)}, s32[8]{0:T(128)}, u32[]{:S(2)}) copy-start(s32[8]{0:T(128)} %param.17) | copy-start | bytes 100
  207.8 190.2 %all-reduce.7.cloned.1.call-start = ((), (), s32[]{:S(2)}) async-start(), calls=%async_computation.3 | async-start | bytes 1572864 | tf_op jit(solution)/shard_map/psum | solution.py:217
  207.9 119.9 %collective-permute-start.5 = (f32[1024,256]{1,0:T(8,128)S(1)}, f32[1024,256]{1,0:T(8,128)}, u32[]{:S(2)}, u32[]{:S(2)}) collective-permute-start(f32[1024,256]{1,0:T(8,128)S(1)} %get-tuple-element.17), channel_id=1, source_target_pairs={{0,12},{4,0},{8,4},{12,8},{1,13},{5,1},{9,5},{13,9},{2,14},{6,2},{... | collective-permute-start | bytes 3145736 | tf_op jit(solution)/shard_map/ppermute | solution.py:139
  209.4 36.0 %collective-permute-start = (f32[1024,128]{1,0:T(8,128)}, f32[1024,128]{1,0:T(8,128)}, u32[]{:S(2)}, u32[]{:S(2)}) collective-permute-start(f32[1024,128]{1,0:T(8,128)} %get-tuple-element.16), channel_id=1, source_target_pairs={{0,4},{4,8},{8,12},{12,0},{1,5},{5,9},{9,13},{13,1},{2,6},{6,10},{... | collective-permute-start | bytes 1572872 | tf_op jit(solution)/shard_map/ppermute | solution.py:139
  209.9 115.9 %collective-permute-start.2 = (f32[1024,128]{1,0:T(8,128)}, f32[1024,128]{1,0:T(8,128)}, u32[]{:S(2)}, u32[]{:S(2)}) collective-permute-start(f32[1024,128]{1,0:T(8,128)} %get-tuple-element.16), channel_id=1, source_target_pairs={{0,12},{4,0},{8,4},{12,8},{1,13},{5,1},{9,5},{13,9},{2,14},{6,2},{... | collective-permute-start | bytes 1572872 | tf_op jit(solution)/shard_map/ppermute | solution.py:139
  213.2 110.8 %collective-permute-start.1 = (f32[1024,128]{1,0:T(8,128)}, f32[1024,128]{1,0:T(8,128)}, u32[]{:S(2)}, u32[]{:S(2)}) collective-permute-start(f32[1024,128]{1,0:T(8,128)} %get-tuple-element.16), channel_id=1, source_target_pairs={{0,8},{4,12},{8,0},{12,4},{1,9},{5,13},{9,1},{13,5},{2,10},{6,14},... | collective-permute-start | bytes 1572872 | tf_op jit(solution)/shard_map/ppermute | solution.py:139
  213.2 131.8 %collective-permute-start.4 = (f32[1024,256]{1,0:T(8,128)S(1)}, f32[1024,256]{1,0:T(8,128)}, u32[]{:S(2)}, u32[]{:S(2)}) collective-permute-start(f32[1024,256]{1,0:T(8,128)S(1)} %get-tuple-element.17), channel_id=1, source_target_pairs={{0,8},{4,12},{8,0},{12,4},{1,9},{5,13},{9,1},{13,5},{2,10},{6,14},... | collective-permute-start | bytes 3145736 | tf_op jit(solution)/shard_map/ppermute | solution.py:139
  222.5 7.2 %copy-start = (f32[1024,256]{1,0:T(8,128)S(1)}, f32[1024,256]{1,0:T(8,128)}, u32[]{:S(2)}) copy-start(f32[1024,256]{1,0:T(8,128)} %fusion.13) | copy-start | bytes 3145732
  223.9 5.8 %copy-start.2 = (f32[1024,256]{1,0:T(8,128)S(1)}, f32[1024,256]{1,0:T(8,128)}, u32[]{:S(2)}) copy-start(f32[1024,256]{1,0:T(8,128)} %copy-done.1) | copy-start | bytes 3145732
  245.4 119.2 %collective-permute-start.3 = (f32[1024,256]{1,0:T(8,128)S(1)}, f32[1024,256]{1,0:T(8,128)}, u32[]{:S(2)}, u32[]{:S(2)}) collective-permute-start(f32[1024,256]{1,0:T(8,128)S(1)} %get-tuple-element.17), channel_id=1, source_target_pairs={{0,4},{4,8},{8,12},{12,0},{1,5},{5,9},{9,13},{13,1},{2,6},{6,10},{... | collective-permute-start | bytes 3145736 | tf_op jit(solution)/shard_map/ppermute | solution.py:139
  350.3 5.4 %copy-start.3 = (f32[2,256,256]{2,1,0:T(8,128)S(1)}, f32[2,256,256]{2,1,0:T(8,128)}, u32[]{:S(2)}) copy-start(f32[2,256,256]{2,1,0:T(8,128)} %param.13) | copy-start | bytes 1572868
  355.6 60.5 %all-gather.4.cloned.1.call-start = ((), (), s32[]{:S(2)}) async-start(), calls=%async_computation | async-start | bytes 1310720 | tf_op jit(solution)/shard_map/all_gather | solution.py:219
  360.4 4.2 copy-start.5
  360.4 4.2 copy-start.6
  364.6 33.4 %copy-start.8 = (f32[1,256,256]{2,1,0:T(8,128)S(1)}, f32[1,256,256]{2,1,0:T(8,128)}, u32[]{:S(2)}) copy-start(f32[1,256,256]{2,1,0:T(8,128)} %param.11) | copy-start | bytes 786436
  399.7 57.7 %all-reduce.5.cloned.1.call-start = ((), (), s32[]{:S(2)}) async-start(), calls=%async_computation.1 | async-start | bytes 1048576 | tf_op jit(solution)/shard_map/psum | solution.py:236
  414.6 42.7 %copy-start.4 = (f32[2,256,256]{2,1,0:T(8,128)S(1)}, f32[2,256,256]{2,1,0:T(8,128)}, u32[]{:S(2)}) copy-start(f32[2,256,256]{2,1,0:T(8,128)} %param.13) | copy-start | bytes 1572868
Sparse Core Ops, SparseCore 0:
  207.9 32.6 all-gather.5
  355.7 42.1 all-reduce.6
  400.1 15.9 all-gather.3
  419.0 38.2 all-reduce.4

commit v2 on v0

v2 whole, which is shorter than its diff:
```python
import functools

import jax
import jax.numpy as jnp
from jax import lax
from jax.experimental import pallas as pl
from jax.experimental.pallas import tpu as pltpu
from jax.sharding import PartitionSpec as P

HIGH = lax.Precision.HIGH


MESH = pl.DeviceIdType.MESH


def gather_kernel(rows_n, f_ref, whole, f_send, f_recv, own):
    row = lax.axis_index("row")
    tall = f_ref.shape[0]
    barrier = pltpu.get_barrier_semaphore()
    for s in range(1, rows_n):
        pl.semaphore_signal(
            barrier, inc=1, device_id={"row": lax.rem(row + s, rows_n)}, device_id_type=MESH
        )
    pl.semaphore_wait(barrier, rows_n - 1)
    place = whole.at[pl.ds(pl.multiple_of(row * tall, tall), tall)]
    sends = []
    for s in range(1, rows_n):
        c = pltpu.make_async_remote_copy(
            src_ref=f_ref,
            dst_ref=place,
            send_sem=f_send.at[s - 1],
            recv_sem=f_recv.at[s - 1],
            device_id={"row": lax.rem(row + s, rows_n)},
            device_id_type=MESH,
        )
        c.start()
        sends.append(c)
    local = pltpu.make_async_copy(f_ref, place, own)
    local.start()
    for c in sends:
        c.wait()
    local.wait()


def gather_first(f, rows_n, number):
    dma = pltpu.SemaphoreType.DMA
    return pl.pallas_call(
        functools.partial(gather_kernel, rows_n),
        out_shape=jax.ShapeDtypeStruct((rows_n * f.shape[0], f.shape[1]), f.dtype),
        in_specs=[pl.BlockSpec(memory_space=pl.ANY)],
        out_specs=pl.BlockSpec(memory_space=pl.ANY),
        scratch_shapes=[dma((rows_n - 1,)), dma((rows_n - 1,)), dma],
        compiler_params=pltpu.CompilerParams(collective_id=number, has_side_effects=True),
    )(f)


def reduce_kernel(rows_n, x_ref, out_ref, inbox, a_send, a_recv, b_send, b_recv):
    row = lax.axis_index("row")
    part = x_ref.shape[0] // rows_n
    barrier = pltpu.get_barrier_semaphore()
    for s in range(1, rows_n):
        pl.semaphore_signal(
            barrier, inc=1, device_id={"row": lax.rem(row + s, rows_n)}, device_id_type=MESH
        )
    pl.semaphore_wait(barrier, rows_n - 1)

    def piece(r):
        return pl.ds(pl.multiple_of(r * part, part), part)

    sends = []
    for s in range(1, rows_n):
        other = lax.rem(row + s, rows_n)
        c = pltpu.make_async_remote_copy(
            src_ref=x_ref.at[piece(other)],
            dst_ref=inbox.at[s - 1],
            send_sem=a_send.at[s - 1],
            recv_sem=a_recv.at[s - 1],
            device_id={"row": other},
            device_id_type=MESH,
        )
        c.start()
        sends.append(c)
    total = x_ref[piece(row), :]
    for s in range(1, rows_n):
        sends[s - 1].wait_recv()
        total = total + inbox[s - 1]
    out_ref[piece(row), :] = total
    back = []
    for s in range(1, rows_n):
        c = pltpu.make_async_remote_copy(
            src_ref=out_ref.at[piece(row)],
            dst_ref=out_ref.at[piece(row)],
            send_sem=b_send.at[s - 1],
            recv_sem=b_recv.at[s - 1],
            device_id={"row": lax.rem(row + s, rows_n)},
            device_id_type=MESH,
        )
        c.start()
        back.append(c)
    for c in sends:
        c.wait_send()
    for c in back:
        c.wait()


def sum_rows(x, rows_n):
    dma = pltpu.SemaphoreType.DMA
    return pl.pallas_call(
        functools.partial(reduce_kernel, rows_n),
        out_shape=jax.ShapeDtypeStruct(x.shape, x.dtype),
        in_specs=[pl.BlockSpec(memory_space=pltpu.VMEM)],
        out_specs=pl.BlockSpec(memory_space=pltpu.VMEM),
        scratch_shapes=[pltpu.VMEM((rows_n - 1, x.shape[0] // rows_n, x.shape[1]), x.dtype)]
        + [dma((rows_n - 1,))] * 4,
        compiler_params=pltpu.CompilerParams(
            collective_id=2, has_side_effects=True, vmem_limit_bytes=24 * 2**20
        ),
    )(x)


def on_device(
    root_inverse,
    root_factor_one,
    diag_inverse_one,
    root_factor_two,
    parent_factor,
    diag_inverse_two,
    root_mask_one,
    root_mask_two,
    parents,
    row_count,
):
    width = parent_factor.shape[1]
    local_rows = root_inverse.shape[0]
    per_one = diag_inverse_one.shape[0]
    per_two = diag_inverse_two.shape[0]
    row_index = lax.axis_index("row")
    col_index = lax.axis_index("col")
    blocks = local_rows // width

    def row_masks(mask, number):
        own = lax.dynamic_slice(mask, (col_index * number, row_index * blocks), (number, blocks))
        return jnp.repeat(own.T.astype(jnp.float32), width, axis=0)

    mask_one = row_masks(root_mask_one, per_one)
    mask_two = row_masks(root_mask_two, per_two)
    one = [
        root_factor_one[:, k * width : (k + 1) * width] * mask_one[:, k : k + 1]
        for k in range(per_one)
    ]
    two = [
        root_factor_two[:, k * width : (k + 1) * width] * mask_two[:, k : k + 1]
        for k in range(per_two)
    ]
    half = width // 2
    early = jnp.concatenate(one + [two[0][:, :half]], axis=1)
    panel = lax.all_gather(root_inverse, "col", axis=1, tiled=True)
    whole_early = gather_first(early, row_count, 0)
    late = jnp.concatenate([two[0][:, half:]] + two[1:], axis=1)
    whole_one = [whole_early[:, k * width : (k + 1) * width] for k in range(per_one)]

    def dot(a, b):
        return jnp.dot(a, b, precision=HIGH, preferred_element_type=jnp.float32)

    def dot_t(a, b):
        return lax.dot_general(
            a, b, (((0,), (0,)), ((), ())), precision=HIGH, preferred_element_type=jnp.float32
        )

    inv_one = [-dot(panel, whole_one[k]) * mask_one[:, k : k + 1] for k in range(per_one)]
    inverse_one = jnp.concatenate(inv_one, axis=1) if per_one > 1 else inv_one[0]
    first = row_index == 0
    excess = [
        dot_t(one[k], inv_one[k]) - jnp.where(first, diag_inverse_one[k], 0.0)
        for k in range(per_one)
    ]
    own_parents = lax.dynamic_slice_in_dim(parents, col_index * per_two, per_two, 0)
    stacked = jnp.concatenate([inverse_one, jnp.concatenate(excess, axis=1)], axis=0)
    stacked, late = lax.optimization_barrier((stacked, late))
    everyone = lax.all_gather(stacked, "col", axis=0, tiled=False)
    whole_late = gather_first(late, row_count, 1)
    everyone, whole_late = lax.optimization_barrier((everyone, whole_late))
    parent_cols, parent_part = [], []
    for k in range(per_two):
        p = own_parents[k]
        own = lax.dynamic_slice(
            everyone,
            (p // per_one, jnp.int32(0), (p % per_one) * width),
            (1, local_rows + width, width),
        )[0]
        parent_cols.append(own[:local_rows])
        parent_part.append(
            dot_t(own[:local_rows], two[k]) - dot(own[local_rows:], parent_factor[k])
        )
    cross = [dot(parent_cols[k], parent_factor[k]) for k in range(per_two)]
    inner = [dot_t(parent_factor[k], parent_part[k]) for k in range(per_two)]
    inv_two = []
    for k in range(per_two):
        if k == 0:
            whole = jnp.concatenate(
                [whole_early[:, per_one * width :], whole_late[:, :half]], axis=1
            )
        else:
            whole = whole_late[:, half + (k - 1) * width : half + k * width]
        inv_two.append(-(dot(panel, whole) + cross[k]) * mask_two[:, k : k + 1])
    diag_part_two = [dot_t(two[k], inv_two[k]) - inner[k] for k in range(per_two)]
    sums = sum_rows(jnp.concatenate(excess + parent_part + diag_part_two, axis=0), row_count)
    sums = sums.reshape(per_one + 2 * per_two, width, width)
    diag_one = -sums[:per_one]
    summed_parent = sums[per_one : per_one + per_two]
    diag_two = diag_inverse_two - sums[per_one + per_two :]
    return (
        inverse_one,
        diag_one,
        jnp.concatenate(inv_two, axis=1),
        -summed_parent,
        diag_two,
    )


def solution(mesh):
    row_count = mesh.shape["row"]
    tall = P(("pole", "row"), "col")
    deep = P(("pole", "col"), None, None)

    def step(*args):
        return on_device(*args, row_count)

    return jax.shard_map(
        step,
        mesh=mesh,
        in_specs=(tall, tall, deep, tall, deep, deep, P(), P(), P()),
        out_specs=(tall, deep, tall, deep, deep),
        check_vma=False,
    )
```

time: 500 us -> 438 us (0.88)
  waiting for transfers between devices: 390 us -> 0.72 us
  Pallas kernels: 0 us -> 331 us
  matrix products: 70.6 us -> 50.7 us
  other arithmetic: 4.16 us -> 9.76 us
    pallas_call x0 -> x3, Pallas kernels: none -> 331 us  [the longest x2 246 us: gather_first(): pl.pallas_call(functools.partial(gather_kernel, rows_n), out_shape=jax.Sh...]
    reduce_scatter x2 -> x0, waiting for transfers between devices: 207 us -> none  [the longest x1 130 us: on_device(): lax.psum_scatter(partial_terms(flat_two), 'row', scatter_dimension=0, til...]
    all_gather x1, waiting for transfers between devices: 108 us -> 0.01 us  [on_device(): panel = lax.all_gather(root_inverse, 'col', axis=1, tiled=True)]
    psum x1 -> x0, waiting for transfers between devices: 61.6 us -> none  [on_device(): diag_one = diag_inverse_one - lax.psum(diag_part, 'row')]
    dot_general x10 -> x14, matrix products: 70.6 us -> 50.7 us  [the longest x7 43.3 us: dot(): return jnp.dot(a, b, precision=HIGH, preferred_element_type=jnp.float32)]
    all_gather x2 -> x1, waiting for transfers between devices: 12.4 us -> 0.02 us  [on_device(): everyone = lax.all_gather(stacked, 'col', axis=0, tiled=False)]
    slice x0 -> x9, local copies, waits for them, and re-layouts: none -> 11.1 us  [the longest x1 5.76 us: on_device(): own[:local_rows]]
    all_gather x0 -> x1, local copies, waits for them, and re-layouts: none -> 7.25 us  [on_device(): everyone = lax.all_gather(stacked, 'col', axis=0, tiled=False)]
  transfers between devices with their start and end apart: 6 -> 2, of which waited for: 5 -> 0; matrix products, arithmetic and copies ran while one was open for 12% -> 2% of each run, Pallas kernels for 0% -> 57%
where the time goes in v2:
time: 438 us; the launch traced here: 434 us
  Pallas kernels  331 us (76%)
  matrix products  50.7 us (12%)
  local copies, waits for them, and re-layouts  23 us (5%)
  between operations  18.3 us (4%)
  other arithmetic  9.76 us (2%)
    pallas_call x2, Pallas kernels, gather_first(): pl.pallas_call(functools.partial(gather_kernel, rows_n), out_shape=jax.Sh...  246 us
    pallas_call x1, Pallas kernels, sum_rows(): pl.pallas_call(functools.partial(reduce_kernel, rows_n), out_shape=jax.Sh...  84.9 us
    dot_general x7, matrix products, dot(): return jnp.dot(a, b, precision=HIGH, preferred_element_type=jnp.float32)  43.3 us
  transfers between devices with their start and end apart: 2, of which 0 were waited for; matrix products, arithmetic and copies ran while one was open for 2% of the time, Pallas kernels for 57%

profile of v2, /device:TPU:0, one launch (start us, length us, event | category | flops | bytes accessed | tf_op | source)
XLA Modules:
  0.0 433.9 jit_solution(543513003713783190)
XLA Ops:
  7.2 0.7 all-gather.4.cloned.1.call-update
  8.0 0.8 convert_bitcast_fusion.1
  8.8 0.8 convert_bitcast_fusion
  10.1 1.9 copy-done.13
  12.2 1.2 pad_maximum_fusion.1.f_ref
  13.5 107.5 %shard_map.128 = f32[4096,384]{1,0:T(8,128)} custom-call(f32[1024,384]{1,0:T(8,128)} %pad_maximum_fusion.1.f_ref), custom_call_target="tpu_custom_call" | custom-call | tf_op jit(solution)/shard_map/pallas_call | solution.py:47
  121.0 1.2 pad_maximum_fusion.2.f_ref
  122.3 18.1 %fusion.11 = f32[256,1024]{1,0:T(8,128)S(1)} fusion(f32[1024,4096]{1,0:T(8,128)} %all-gather.4.cloned.1.call-done, f32[4096,384]{1,0:T(8,128)} %shard_map.128, f32[1024]{0:T(1024)S(1)} %bitcast.99), kind=kOutput, calls=%fused_computation.12 | convolution fusion | flops 6442975232 | bytes 22024192 | tf_op jit(solution)/shard_map/dot_general | solution.py:163
  140.4 1.7 constant_dynamic-update-slice_fusion.2
  142.1 1.1 copy.21
  143.2 1.2 pad_maximum_fusion.3
  144.5 0.6 fusion.58
  149.0 1.3 copy.26
  150.3 138.8 %shard_map.129 = f32[4096,384]{1,0:T(8,128)} custom-call(f32[1024,384]{1,0:T(8,128)} %pad_maximum_fusion.2.f_ref), custom_call_target="tpu_custom_call" | custom-call | tf_op jit(solution)/shard_map/pallas_call | solution.py:47
  289.2 7.2 %reshape.37 = f32[4,1280,256]{1,0,2:T(4,128)} reshape(f32[5120,256]{0,1:T(8,128)} %all-gather.6.cloned.1.call-done) | data formatting | bytes 10485760 | tf_op jit(solution)/shard_map/all_gather | solution.py:180
  296.4 5.8 %constant_dynamic-slice_fusion = (f32[1,1024,256]{1,0,2:T(1,128)S(1)}, f32[1,1024,256]{1,0,2:T(1,128)S(1)}) fusion(f32[4,1280,256]{1,0,2:T(4,128)} %reshape.37, s32[]{:T(128)S(6)} %select_n.47, s32[]{:T(128)S(6)} %select_n.46), kind=kLoop, calls=%fused_computation.68 | loop fusion | bytes 4194312 | tf_op jit(solution)/shard_map/slice | solution.py:193
  302.2 1.4 fusion.29
  303.6 1.4 fusion.32
  305.1 1.8 slice-done.4
  306.9 11.4 %fusion.17 = f32[1024,256]{1,0:T(8,128)} fusion(f32[1024,4096]{1,0:T(8,128)} %all-gather.4.cloned.1.call-done, f32[4096,128]{1,0:T(8,128)S(1)} %slice-done.5, f32[4096,128]{1,0:T(8,128)S(1)} %slice-done.4), kind=kOutput, calls=%fused_computation.14 | convolution fusion | flops 6443499520 | bytes 22020096 | tf_op jit(solution)/shard_map/dot_general | solution.py:163
  318.3 2.7 fusion.23
  321.1 9.2 %fusion.14 = f32[1024,256]{1,0:T(8,128)S(1)} fusion(f32[1024,4096]{1,0:T(8,128)S(1)} %bitcast.93, f32[4096,384]{1,0:T(8,128)} %shard_map.129), kind=kOutput, calls=%fused_computation.13 | convolution fusion | flops 6442450944 | bytes 22020096 | tf_op jit(solution)/shard_map/dot_general | solution.py:163
  330.3 1.1 fusion.21
  331.5 1.0 fusion.60
  332.6 1.0 fusion.59
  333.6 1.6 pad_maximum_fusion
  335.2 2.9 constant_dynamic-slice_fusion.2
  338.1 0.4 constant_dynamic-update-slice_fusion.1
  339.7 84.9 %shard_map.130 = f32[1280,256]{1,0:T(8,128)S(1)} custom-call(f32[1280,256]{1,0:T(8,128)S(1)} %fusion.25.x_ref), custom_call_target="tpu_custom_call" | custom-call | tf_op jit(solution)/shard_map/pallas_call | solution.py:108
  424.6 0.7 negate_bitcast_fusion
  425.3 0.9 fusion.55
  426.2 0.9 sub.26
  (62 shorter events, 2.3 us)
Async XLA Ops:
  7.2 2.5 copy-start.10
  7.2 115.1 %all-gather.4.cloned.1.call-start = ((), (), s32[]{:S(2)}) async-start(), calls=%async_computation | async-start | bytes 20971520 | tf_op jit(solution)/shard_map/all_gather | solution.py:157
  7.9 281.2 %all-gather.6.cloned.1.call-start = ((), (), s32[]{:S(2)}) async-start(), calls=%async_computation.1 | async-start | bytes 6553600 | tf_op jit(solution)/shard_map/all_gather | solution.py:180
  10.0 2.2 copy-start.3
  10.0 111.0 %copy-start = (f32[1024,256]{1,0:T(8,128)}, f32[1024,256]{1,0:T(8,128)S(1)}, u32[]{:S(2)}) copy-start(f32[1024,256]{1,0:T(8,128)S(1)} %get-tuple-element.27) | copy-start | bytes 3145732
  10.0 2.0 copy-start.13
  122.3 18.1 %copy-start.15 = (f32[1,256,256]{2,1,0:T(8,128)S(1)}, f32[1,256,256]{2,1,0:T(8,128)}, u32[]{:S(2)}) copy-start(f32[1,256,256]{2,1,0:T(8,128)} %param.11) | copy-start | bytes 786436
  143.2 1.2 copy-start.16
  296.4 5.8 %copy-start.1 = (f32[1024,256]{1,0:T(8,128)S(1)}, f32[1024,256]{1,0:T(8,128)}, u32[]{:S(2)}) copy-start(f32[1024,256]{1,0:T(8,128)} %copy-done) | copy-start | bytes 3145732
  296.4 7.2 %copy-start.4 = (f32[1024,256]{1,0:T(8,128)S(1)}, f32[1024,256]{1,0:T(8,128)}, u32[]{:S(2)}) copy-start(f32[1024,256]{1,0:T(8,128)} %copy-done.3) | copy-start | bytes 3145732
  302.2 2.9 copy-start.6
  302.2 2.9 copy-start.8
  302.2 2.9 slice-start.5
  303.6 17.4 %slice-start = ((s8[16777216]{0:T(1024)(128)(4,1)}), s8[4194304]{0:T(1024)(128)(4,1)S(1)}, s32[]{:S(2)}) async-start(s8[16777216]{0:T(1024)(128)(4,1)} %bitcast.92), calls=%async_computation.2 | async-start | bytes 8388608
  305.1 1.8 slice-start.4
  306.9 14.2 %slice-start.1 = ((s8[16777216]{0:T(1024)(128)(4,1)}), s8[4194304]{0:T(1024)(128)(4,1)S(1)}, s32[]{:S(2)}) async-start(s8[16777216]{0:T(1024)(128)(4,1)} %bitcast.92), calls=%async_computation.3 | async-start | bytes 8388608
  306.9 14.2 %slice-start.2 = ((s8[16777216]{0:T(1024)(128)(4,1)}), s8[4194304]{0:T(1024)(128)(4,1)S(1)}, s32[]{:S(2)}) async-start(s8[16777216]{0:T(1024)(128)(4,1)} %bitcast.92), calls=%async_computation.4 | async-start | bytes 8388608
  306.9 14.2 %slice-start.3 = ((s8[16777216]{0:T(1024)(128)(4,1)}), s8[4194304]{0:T(1024)(128)(4,1)S(1)}, s32[]{:S(2)}) async-start(s8[16777216]{0:T(1024)(128)(4,1)} %bitcast.92), calls=%async_computation.5 | async-start | bytes 8388608
  321.1 9.2 %copy-start.7 = (f32[1,1024,256]{1,0,2:T(1,128)S(1)}, f32[1,1024,256]{1,0,2:T(1,128)}, u32[]{:S(2)}) copy-start(f32[1,1024,256]{1,0,2:T(1,128)} %copy-done.6) | copy-start | bytes 3145732
  321.1 9.2 %copy-start.9 = (f32[2,256,256]{2,1,0:T(8,128)S(1)}, f32[2,256,256]{2,1,0:T(8,128)}, u32[]{:S(2)}) copy-start(f32[2,256,256]{2,1,0:T(8,128)} %param.13) | copy-start | bytes 1572868
  330.3 1.2 copy-start.2
  330.3 2.3 copy-start.5
  333.6 4.5 %copy-start.12 = (f32[256,256]{1,0:T(8,128)S(1)}, f32[256,256]{1,0:T(8,128)}, u32[]{:S(2)}) copy-start(f32[256,256]{1,0:T(8,128)} %fusion.32) | copy-start | bytes 786436
  335.2 3.3 copy-start.11
  339.7 86.5 %copy-start.14 = (f32[2,256,256]{2,1,0:T(8,128)S(1)}, f32[2,256,256]{2,1,0:T(8,128)}, u32[]{:S(2)}) copy-start(f32[2,256,256]{2,1,0:T(8,128)} %param.14) | copy-start | bytes 1572868
Sparse Core Ops, SparseCore 0:
  9.6 108.6 all-gather.3
  144.5 74.1 all-gather.5

commit v3 on v2

--- a/solution.py
+++ b/solution.py
@@ -64,43 +64,46 @@
         )
     pl.semaphore_wait(barrier, rows_n - 1)
 
-    def piece(r):
-        return pl.ds(pl.multiple_of(r * part, part), part)
-
-    sends = []
-    for s in range(1, rows_n):
+    half = part // 2
+
+    def piece(r, h):
+        return pl.ds(pl.multiple_of(r * part + h * half, half), half)
+
+    def there(s, h):
         other = lax.rem(row + s, rows_n)
-        c = pltpu.make_async_remote_copy(
-            src_ref=x_ref.at[piece(other)],
-            dst_ref=inbox.at[s - 1],
-            send_sem=a_send.at[s - 1],
-            recv_sem=a_recv.at[s - 1],
+        return pltpu.make_async_remote_copy(
+            src_ref=x_ref.at[piece(other, h)],
+            dst_ref=inbox.at[h, s - 1],
+            send_sem=a_send.at[h, s - 1],
+            recv_sem=a_recv.at[h, s - 1],
             device_id={"row": other},
             device_id_type=MESH,
         )
-        c.start()
-        sends.append(c)
-    total = x_ref[piece(row), :]
-    for s in range(1, rows_n):
-        sends[s - 1].wait_recv()
-        total = total + inbox[s - 1]
-    out_ref[piece(row), :] = total
-    back = []
-    for s in range(1, rows_n):
-        c = pltpu.make_async_remote_copy(
-            src_ref=out_ref.at[piece(row)],
-            dst_ref=out_ref.at[piece(row)],
-            send_sem=b_send.at[s - 1],
-            recv_sem=b_recv.at[s - 1],
+
+    def back(s, h):
+        return pltpu.make_async_remote_copy(
+            src_ref=out_ref.at[piece(row, h)],
+            dst_ref=out_ref.at[piece(row, h)],
+            send_sem=b_send.at[h, s - 1],
+            recv_sem=b_recv.at[h, s - 1],
             device_id={"row": lax.rem(row + s, rows_n)},
             device_id_type=MESH,
         )
-        c.start()
-        back.append(c)
-    for c in sends:
-        c.wait_send()
-    for c in back:
-        c.wait()
+
+    pairs = [(s, h) for h in range(2) for s in range(1, rows_n)]
+    for s, h in pairs:
+        there(s, h).start()
+    for h in range(2):
+        total = x_ref[piece(row, h), :]
+        for s in range(1, rows_n):
+            there(s, h).wait_recv()
+            total = total + inbox[h, s - 1]
+        out_ref[piece(row, h), :] = total
+        for s in range(1, rows_n):
+            back(s, h).start()
+    for s, h in pairs:
+        there(s, h).wait_send()
+        back(s, h).wait()
 
 
 def sum_rows(x, rows_n):
@@ -110,8 +113,8 @@
         out_shape=jax.ShapeDtypeStruct(x.shape, x.dtype),
         in_specs=[pl.BlockSpec(memory_space=pltpu.VMEM)],
         out_specs=pl.BlockSpec(memory_space=pltpu.VMEM),
-        scratch_shapes=[pltpu.VMEM((rows_n - 1, x.shape[0] // rows_n, x.shape[1]), x.dtype)]
-        + [dma((rows_n - 1,))] * 4,
+        scratch_shapes=[pltpu.VMEM((2, rows_n - 1, x.shape[0] // rows_n // 2, x.shape[1]), x.dtype)]
+        + [dma((2, rows_n - 1))] * 4,
         compiler_params=pltpu.CompilerParams(
             collective_id=2, has_side_effects=True, vmem_limit_bytes=24 * 2**20
         ),
@@ -177,7 +180,7 @@
     own_parents = lax.dynamic_slice_in_dim(parents, col_index * per_two, per_two, 0)
     stacked = jnp.concatenate([inverse_one, jnp.concatenate(excess, axis=1)], axis=0)
     stacked, late = lax.optimization_barrier((stacked, late))
-    everyone = lax.all_gather(stacked, "col", axis=0, tiled=False)
+    everyone = lax.all_gather(stacked, "col", axis=0, tiled=True)
     whole_late = gather_first(late, row_count, 1)
     everyone, whole_late = lax.optimization_barrier((everyone, whole_late))
     parent_cols, parent_part = [], []
@@ -185,9 +188,9 @@
         p = own_parents[k]
         own = lax.dynamic_slice(
             everyone,
-            (p // per_one, jnp.int32(0), (p % per_one) * width),
-            (1, local_rows + width, width),
-        )[0]
+            ((p // per_one) * (local_rows + width), (p % per_one) * width),
+            (local_rows + width, width),
+        )
         parent_cols.append(own[:local_rows])
         parent_part.append(
             dot_t(own[:local_rows], two[k]) - dot(own[local_rows:], parent_factor[k])

time: 438 us -> 426 us (0.973)
  local copies, waits for them, and re-layouts: 23 us -> 6.85 us
  matrix products: 50.7 us -> 57.3 us
    slice x2 -> x0, local copies, waits for them, and re-layouts: 8.61 us -> none  [the longest x1 5.76 us: on_device(): own[:local_rows]]
    all_gather x1 -> x0, local copies, waits for them, and re-layouts: 7.25 us -> none  [on_device(): everyone = lax.all_gather(stacked, 'col', axis=0, tiled=False)]
  transfers between devices with their start and end apart: 2 -> 2, of which waited for: 0 -> 0; matrix products, arithmetic and copies ran while one was open for 2% -> 2% of each run, Pallas kernels for 57% -> 58%
where the time goes in v3:
time: 426 us; the launch traced here: 425 us
  Pallas kernels  335 us (79%)
  matrix products  57.3 us (13%)
  between operations  15.7 us (4%)
  other arithmetic  9.71 us (2%)
  local copies, waits for them, and re-layouts  6.85 us (2%)
    pallas_call x2, Pallas kernels, gather_first(): pl.pallas_call(functools.partial(gather_kernel, rows_n), out_shape=jax.Sh...  246 us
    pallas_call x1, Pallas kernels, sum_rows(): pl.pallas_call(functools.partial(reduce_kernel, rows_n), out_shape=jax.Sh...  88.4 us
    dot_general x7, matrix products, dot(): return jnp.dot(a, b, precision=HIGH, preferred_element_type=jnp.float32)  46.7 us
    dot_general x7, matrix products, dot_t(): lax.dot_general(a, b, (((0,), (0,)), ((), ())), precision=HIGH, preferred...  10.6 us
  transfers between devices with their start and end apart: 2, of which 0 were waited for; matrix products, arithmetic and copies ran while one was open for 2% of the time, Pallas kernels for 58%

profile of v3, /device:TPU:0, one launch (start us, length us, event | category | flops | bytes accessed | tf_op | source)
XLA Modules:
  0.0 425.2 jit_solution(1755184278877760849)
XLA Ops:
  7.2 0.7 all-gather.3.cloned.1.call-update
  8.0 0.8 convert_bitcast_fusion.1
  8.8 0.8 convert_bitcast_fusion
  10.1 1.9 copy-done.8
  12.2 1.2 pad_maximum_fusion.1.f_ref
  13.5 107.5 %shard_map.128 = f32[4096,384]{1,0:T(8,128)} custom-call(f32[1024,384]{1,0:T(8,128)} %pad_maximum_fusion.1.f_ref), custom_call_target="tpu_custom_call" | custom-call | tf_op jit(solution)/shard_map/pallas_call | solution.py:47
  121.0 1.2 pad_maximum_fusion.2.f_ref
  122.3 18.2 %fusion.11 = f32[256,1024]{1,0:T(8,128)S(1)} fusion(f32[1024,4096]{1,0:T(8,128)} %all-gather.3.cloned.1.call-done, f32[4096,384]{1,0:T(8,128)} %shard_map.128, f32[1024]{0:T(1024)S(1)} %bitcast.77), kind=kOutput, calls=%fused_computation.12 | convolution fusion | flops 6442975232 | bytes 22024192 | tf_op jit(solution)/shard_map/dot_general | solution.py:166
  140.5 1.7 constant_dynamic-update-slice_fusion.2
  142.2 1.1 copy.21
  143.3 1.1 pad_maximum_fusion.3
  144.5 0.6 fusion.58
  146.4 1.3 copy.26
  147.7 138.8 %shard_map.129 = f32[4096,384]{1,0:T(8,128)} custom-call(f32[1024,384]{1,0:T(8,128)} %pad_maximum_fusion.2.f_ref), custom_call_target="tpu_custom_call" | custom-call | tf_op jit(solution)/shard_map/pallas_call | solution.py:47
  286.6 3.0 fusion.29
  289.6 3.0 fusion.32
  292.6 1.6 slice-done.4
  294.2 11.6 %fusion.17 = f32[1024,256]{1,0:T(8,128)} fusion(f32[1024,4096]{1,0:T(8,128)} %all-gather.3.cloned.1.call-done, f32[4096,128]{1,0:T(8,128)S(1)} %slice-done.5, f32[4096,128]{1,0:T(8,128)S(1)} %slice-done.4), kind=kOutput, calls=%fused_computation.14 | convolution fusion | flops 6443499520 | bytes 22020096 | tf_op jit(solution)/shard_map/dot_general | solution.py:166
  305.8 2.7 fusion.23
  308.6 9.1 %fusion.14 = f32[1024,256]{1,0:T(8,128)S(1)} fusion(f32[1024,4096]{1,0:T(8,128)S(1)} %bitcast.71, f32[4096,384]{1,0:T(8,128)} %shard_map.129), kind=kOutput, calls=%fused_computation.13 | convolution fusion | flops 6442450944 | bytes 22020096 | tf_op jit(solution)/shard_map/dot_general | solution.py:166
  317.7 2.5 fusion.21
  320.2 1.0 fusion.60
  321.3 1.0 fusion.59
  322.3 1.6 pad_maximum_fusion
  323.9 1.3 constant_dynamic-update-slice_fusion.1
  325.3 1.3 constant_dynamic-update-slice_fusion
  326.6 0.4 fusion.27
  327.0 0.4 fusion.25.x_ref
  327.4 88.4 %shard_map.130 = f32[1280,256]{1,0:T(8,128)S(1)} custom-call(f32[1280,256]{1,0:T(8,128)S(1)} %fusion.25.x_ref), custom_call_target="tpu_custom_call" | custom-call | tf_op jit(solution)/shard_map/pallas_call | solution.py:111
  415.9 0.7 negate_bitcast_fusion
  416.6 0.9 fusion.55
  417.5 0.9 sub.26
  (49 shorter events, 1.1 us)
Async XLA Ops:
  7.2 2.5 copy-start.5
  7.2 115.1 %all-gather.3.cloned.1.call-start = ((), (), s32[]{:S(2)}) async-start(), calls=%async_computation | async-start | bytes 20971520 | tf_op jit(solution)/shard_map/all_gather | solution.py:160
  7.9 278.7 %all-gather.5.cloned.1.call-start = ((), (), s32[]{:S(2)}) async-start(), calls=%async_computation.1 | async-start | bytes 6553600 | tf_op jit(solution)/shard_map/all_gather | solution.py:183
  10.0 2.2 copy-start.2
  10.0 111.0 %copy-start = (f32[1024,256]{1,0:T(8,128)}, f32[1024,256]{1,0:T(8,128)S(1)}, u32[]{:S(2)}) copy-start(f32[1024,256]{1,0:T(8,128)S(1)} %get-tuple-element.23) | copy-start | bytes 3145732
  10.0 2.0 copy-start.8
  122.3 18.2 %copy-start.10 = (f32[1,256,256]{2,1,0:T(8,128)S(1)}, f32[1,256,256]{2,1,0:T(8,128)}, u32[]{:S(2)}) copy-start(f32[1,256,256]{2,1,0:T(8,128)} %param.11) | copy-start | bytes 786436
  143.3 1.2 copy-start.11
  286.6 6.0 %slice-start.5 = ((f32[4096,384]{1,0:T(8,128)}), f32[4096,128]{1,0:T(8,128)S(1)}, s32[]{:S(2)}) async-start(f32[4096,384]{1,0:T(8,128)} %shard_map.129), calls=%async_computation.7 | async-start | bytes 4194304 | tf_op jit(solution)/shard_map/slice | solution.py:204
  289.6 18.9 %slice-start = ((s8[16777216]{0:T(1024)(128)(4,1)}), s8[4194304]{0:T(1024)(128)(4,1)S(1)}, s32[]{:S(2)}) async-start(s8[16777216]{0:T(1024)(128)(4,1)} %bitcast.70), calls=%async_computation.2 | async-start | bytes 8388608
  292.6 1.6 slice-start.4
  294.2 14.3 %slice-start.1 = ((s8[16777216]{0:T(1024)(128)(4,1)}), s8[4194304]{0:T(1024)(128)(4,1)S(1)}, s32[]{:S(2)}) async-start(s8[16777216]{0:T(1024)(128)(4,1)} %bitcast.70), calls=%async_computation.3 | async-start | bytes 8388608
  294.2 14.3 %slice-start.2 = ((s8[16777216]{0:T(1024)(128)(4,1)}), s8[4194304]{0:T(1024)(128)(4,1)S(1)}, s32[]{:S(2)}) async-start(s8[16777216]{0:T(1024)(128)(4,1)} %bitcast.70), calls=%async_computation.4 | async-start | bytes 8388608
  294.2 14.3 %slice-start.3 = ((s8[16777216]{0:T(1024)(128)(4,1)}), s8[4194304]{0:T(1024)(128)(4,1)S(1)}, s32[]{:S(2)}) async-start(s8[16777216]{0:T(1024)(128)(4,1)} %bitcast.70), calls=%async_computation.5 | async-start | bytes 8388608
  308.6 9.1 %copy-start.4 = (f32[2,256,256]{2,1,0:T(8,128)S(1)}, f32[2,256,256]{2,1,0:T(8,128)}, u32[]{:S(2)}) copy-start(f32[2,256,256]{2,1,0:T(8,128)} %param.13) | copy-start | bytes 1572868
  317.7 2.5 copy-start.1
  317.7 3.5 copy-start.3
  322.3 1.6 copy-start.7
  322.3 2.9 copy-start.6
  327.4 90.1 %copy-start.9 = (f32[2,256,256]{2,1,0:T(8,128)S(1)}, f32[2,256,256]{2,1,0:T(8,128)}, u32[]{:S(2)}) copy-start(f32[2,256,256]{2,1,0:T(8,128)} %param.14) | copy-start | bytes 1572868
Sparse Core Ops, SparseCore 0:
  9.6 108.6 all-gather.2
  144.6 74.1 all-gather.4
